TPU v7x, 32 devices: a whole 2x2x4 slice. The times are simulated.
32 devices in a mesh: groups: 2 (over y), seq: 4 (over z), dp: 4 (over x, core).
Axes of the slice: x: 2, y: 2, z: 4, core: 2. Of those that a mesh axis runs over, the one named last changes fastest.
Arguments:
- inputs: bfloat16 [8, 4096, 448], P(('groups', 'dp'), 'seq'), parts along dimension 0, may hold values from -6 to 6
- cotangent: bfloat16 [8, 4096, 448], P(('groups', 'dp'), 'seq'), parts along dimension 0, may hold values from -6 to 6
- first_weight_matrix: bfloat16 [3, 448, 448], P(None, None, 'dp'), may hold values from -0.15625 to 0.15625
- weight_two: bfloat16 [3, 448, 448], P(None, None, 'dp'), may hold values from -0.15625 to 0.15625
Outputs:
- input_grad: bfloat16 [8, 4096, 448], P(('groups', 'dp'), 'seq'), parts along dimension 0
- grad_one: float32 [6, 448, 448], P('groups', None, 'dp'), parts along dimension 0
- grad_two: float32 [6, 448, 448], P('groups', None, 'dp'), parts along dimension 0
There are 2 independent parts, one for each index of `groups`. A program takes and returns all parts, laid end to end along the dimension named above; an argument that names none is the same for every part. Nothing has to cross between parts.
All inputs are finite; a program needn't handle non-finite values.
Results may differ from a plain program's by a relative error of at most 0.012.
Values may be sent and summed in bfloat16 or wider, within the bound.
A program may use at most 64 MiB of HBM per device.

v0:
```python
import math

import jax
import jax.numpy as jnp
from jax import lax
from jax.sharding import PartitionSpec as P


def shifted(block, axis, distance):
    devices = range(lax.axis_size(axis))
    route = [(i - distance, i) for i in devices if i - distance in devices]
    return lax.ppermute(block, axis, route)


def gelu_slope(value):
    return jax.vjp(jax.nn.gelu, value)[1](jnp.ones_like(value))[0]


def outer_terms(left, right, factor):
    product = lax.dot_general(
        left, right, (((0,), (0,)), ((), ())), preferred_element_type=jnp.float32
    )
    return product * factor


def back_product(tap, weight):
    return lax.dot_general(
        tap, weight, (((1,), (1,)), ((), ())), preferred_element_type=jnp.float32
    )


def on_device(inputs, cotangent, first_weight_matrix, weight_two):
    chans = inputs.shape[2]
    rows = inputs.shape[0] * inputs.shape[1]
    factor = 1.0 / math.sqrt(
        inputs.shape[0] * lax.axis_size("dp") * inputs.shape[1] * lax.axis_size("seq")
    )
    full_one = lax.all_gather(first_weight_matrix, "dp", axis=2, tiled=True)
    flat_in = inputs.reshape(rows, chans)
    inputs_f = flat_in.astype(jnp.float32)
    input_activation = jax.nn.gelu(inputs_f).astype(jnp.bfloat16)
    act_before = shifted(input_activation, "seq", 2)
    act_after = shifted(input_activation, "seq", -2)
    flat_cot = cotangent.reshape(rows, chans)
    cot_later = shifted(flat_cot, "seq", -4)
    cot_earlier = shifted(flat_cot, "seq", 4)
    preactivation = jnp.dot(act_before, full_one[0], preferred_element_type=jnp.float32)
    preactivation = preactivation + jnp.dot(
        input_activation, full_one[1], preferred_element_type=jnp.float32
    )
    preactivation = preactivation + jnp.dot(
        act_after, full_one[2], preferred_element_type=jnp.float32
    )
    hidden_f = (inputs_f + preactivation).astype(jnp.bfloat16).astype(jnp.float32)
    act_one = jax.nn.gelu(hidden_f).astype(jnp.bfloat16)
    full_two = lax.all_gather(weight_two, "dp", axis=2, tiled=True)
    second_layer_taps = (cot_later, flat_cot, cot_earlier)
    delta_one = back_product(second_layer_taps[0], full_two[0])
    delta_one = delta_one + back_product(second_layer_taps[1], full_two[1])
    delta_one = delta_one + back_product(second_layer_taps[2], full_two[2])
    middle_gradient = (flat_cot.astype(jnp.float32) + gelu_slope(hidden_f) * delta_one).astype(
        jnp.bfloat16
    )
    part_two = jnp.stack(
        [outer_terms(act_one, second_layer_taps[k], factor) for k in range(3)]
    ).astype(jnp.bfloat16)
    grad_two = lax.psum(
        lax.psum_scatter(part_two, "dp", scatter_dimension=2, tiled=True).astype(jnp.float32), "seq"
    )
    grad_later = shifted(middle_gradient, "seq", -2)
    grad_earlier = shifted(middle_gradient, "seq", 2)
    first_layer_taps = (grad_later, middle_gradient, grad_earlier)
    delta_zero = back_product(first_layer_taps[0], full_one[0])
    delta_zero = delta_zero + back_product(first_layer_taps[1], full_one[1])
    delta_zero = delta_zero + back_product(first_layer_taps[2], full_one[2])
    input_grad = (middle_gradient.astype(jnp.float32) + gelu_slope(inputs_f) * delta_zero).astype(
        jnp.bfloat16
    )
    part_one = jnp.stack(
        [outer_terms(input_activation, first_layer_taps[k], factor) for k in range(3)]
    ).astype(jnp.bfloat16)
    grad_one = lax.psum(
        lax.psum_scatter(part_one, "dp", scatter_dimension=2, tiled=True).astype(jnp.float32), "seq"
    )
    return (input_grad.reshape(inputs.shape), grad_one, grad_two)


def solution(mesh):
    placed = (
        P(("groups", "dp"), "seq", None),
        P(("groups", "dp"), "seq", None),
        P(None, None, "dp"),
        P(None, None, "dp"),
    )
    return jax.shard_map(
        on_device,
        mesh=mesh,
        in_specs=placed,
        out_specs=(
            P(("groups", "dp"), "seq", None),
            P("groups", None, "dp"),
            P("groups", None, "dp"),
        ),
        check_vma=False,
    )
```

profile of v0, /device:TPU:0, one launch (start us, length us, event | category | flops | bytes accessed | tf_op | source)
XLA Modules:
  0.0 242.5 jit_solution(234301999639612765)
XLA Ops:
  7.2 0.0 all-gather.3.cloned.1.call-start
  7.2 2.2 copy.9
  9.4 0.0 all-gather.3.cloned.1.call-update
  9.4 0.0 all-gather.5.cloned.1.call-start
  9.5 2.1 copy.13
  11.6 0.0 all-gather.5.cloned.1.call-update
  11.6 0.0 reduce-scatter.9.cloned.1.call-start
  11.7 1.6 fusion.26
  13.2 6.9 %collective-permute-start = (bf16[1024,448]{0,1:T(8,128)(2,1)}, bf16[1024,448]{0,1:T(8,128)(2,1)}, u32[]{:S(2)}, u32[]{:S(2)}) collective-permute-start(bf16[1024,448]{0,1:T(8,128)(2,1)} %fusion.26), channel_id=1, source_target_pairs={{0,8},{4,12},{1,9},{5,13},{2,10},{6,14},{3,11},{7,15},{16,24},{20,... | collective-permute-start | bytes 2752520 | tf_op jit(solution)/shard_map/ppermute | solution.py:12
  20.1 1.3 collective-permute-start.1
  21.4 1.6 collective-permute-start.2
  23.0 11.0 %all-gather.3.cloned.1.call-done = bf16[3,448,448]{1,0,2:T(4,128)(2,1)} async-done(((bf16[3,448,112]{1,0,2:T(4,128)(2,1)}), bf16[3,448,448]{1,0,2:T(4,128)(2,1)}) %all-gather.3.cloned.1.call-update) | async-done | bytes 1204240 | tf_op jit(solution)/shard_map/all_gather | solution.py:38
  34.0 6.1 %fusion.88 = (bf16[1,448,448]{1,0,2:T(2,128)(2,1)S(1)}, bf16[1,448,448]{1,0,2:T(2,128)(2,1)S(1)}, bf16[1,448,448]{1,0,2:T(2,128)(2,1)}) fusion(bf16[3,448,448]{1,0,2:T(4,128)(2,1)} %all-gather.3.cloned.1.call-done), kind=kLoop, calls=%fused_computation.93 | loop fusion | bytes 2408448 | tf_op jit(solution)/shard_map/slice | solution.py:52
  40.1 17.2 %all-gather.5.cloned.1.call-done = bf16[3,448,448]{1,0,2:T(4,128)(2,1)} async-done(((bf16[3,448,112]{1,0,2:T(4,128)(2,1)}), bf16[3,448,448]{1,0,2:T(4,128)(2,1)}) %all-gather.5.cloned.1.call-update) | async-done | bytes 1204240 | tf_op jit(solution)/shard_map/all_gather | solution.py:56
  57.3 6.3 %fusion.87 = (bf16[1,448,448]{1,0,2:T(2,128)(2,1)}, bf16[1,448,448]{1,0,2:T(2,128)(2,1)}, bf16[1,448,448]{1,0,2:T(2,128)(2,1)}) fusion(bf16[3,448,448]{1,0,2:T(4,128)(2,1)} %all-gather.5.cloned.1.call-done), kind=kLoop, calls=%fused_computation.92 | loop fusion | bytes 2408448 | tf_op jit(solution)/shard_map/slice | solution.py:60
  63.6 2.4 copy.21
  66.0 2.0 copy.22
  68.0 1.9 copy.23
  69.9 3.5 %copy.24 = bf16[1,448,448]{2,1,0:T(8,128)(2,1)} copy(bf16[1,448,448]{1,0,2:T(2,128)(2,1)} %get-tuple-element.7) | data formatting | bytes 802816
  73.4 1.3 copy.25
  74.7 1.0 fusion.46
  75.7 3.1 %fusion.57 = f32[1024,448]{0,1:T(8,128)} fusion(bf16[1,448,448]{2,1,0:T(8,128)(2,1)S(1)} %copy.25, bf16[1,1024,448]{1,2,0:T(8,128)(2,1)} %param.5), kind=kOutput, calls=%fused_computation.71 | convolution fusion | flops 411041792 | bytes 3153920 | tf_op jit(solution)/shard_map/dot_general | solution.py:27
  78.8 1.9 fusion.74
  80.8 2.1 fusion.27
  82.8 0.0 copy-start.17
  82.8 2.3 fusion.40
  85.2 2.0 fusion.41
  87.2 0.2 pad_maximum_fusion.1
  87.4 1.8 copy.19
  89.2 2.5 %reshape.22 = bf16[448,1344]{1,0:T(8,128)(2,1)} reshape(bf16[448,3,448]{2,1,0:T(4,128)(2,1)S(1)} %bitcast.119) | data formatting | bytes 2408448
  91.7 0.0 reduce-scatter.9.cloned.1.call-update
  91.8 0.2 reduce-scatter.7.cloned.1.call-start
  92.0 3.2 %fusion.59 = f32[1024,448]{0,1:T(8,128)} fusion(bf16[1024,448]{0,1:T(8,128)(2,1)} %collective-permute-done.2, bf16[1,448,448]{2,1,0:T(8,128)(2,1)S(1)} %copy-done.10), kind=kOutput, calls=%fused_computation.73 | convolution fusion | flops 411041792 | bytes 3153920 | tf_op jit(solution)/shard_map/dot_general | solution.py:27
  95.2 1.3 copy.26
  96.5 4.2 %fusion.17 = bf16[1024,448]{0,1:T(8,128)(2,1)S(1)} fusion(bf16[1024,448]{0,1:T(8,128)(2,1)} %copy-done.17, f32[1024,448]{0,1:T(8,128)} %fusion.59, f32[1024,448]{0,1:T(8,128)S(1)} %copy-done.7, bf16[1024,448]{0,1:T(8,128)(2,1)} %collective-permute-done.2, bf16[1,448,448]{2,1,0:T(8,128)(2,1)S(1)} %copy.26, bf16[1,1024,448]{1,2,0:T(8,128)(2,1)} %param.5), kind=kOutput, calls=%fused_computation.27 | convolution fusion | flops 422051840 | bytes 7741440 | tf_op jit(solution)/shard_map/dot_general | solution.py:27
  100.7 4.5 %collective-permute-start.4 = (bf16[1024,448]{0,1:T(8,128)(2,1)S(1)}, bf16[1024,448]{0,1:T(8,128)(2,1)S(1)}, u32[]{:S(2)}, u32[]{:S(2)}) collective-permute-start(bf16[1024,448]{0,1:T(8,128)(2,1)S(1)} %fusion.17), channel_id=1, source_target_pairs={{0,8},{4,12},{1,9},{5,13},{2,10},{6,14},{3,11},{7,15},{16,24},{20,... | collective-permute-start | bytes 2752520 | tf_op jit(solution)/shard_map/ppermute | solution.py:12
  105.2 1.3 collective-permute-start.3
  106.5 0.8 fusion.43
  107.4 17.8 %collective-permute-done.4 = bf16[1024,448]{0,1:T(8,128)(2,1)S(1)} collective-permute-done((bf16[1024,448]{0,1:T(8,128)(2,1)S(1)}, bf16[1024,448]{0,1:T(8,128)(2,1)S(1)}, u32[]{:S(2)}, u32[]{:S(2)}) %collective-permute-start.4) | collective-permute-done | bytes 917536 | tf_op jit(solution)/shard_map/ppermute | solution.py:12
  125.2 0.8 fusion.42
  126.0 0.1 copy-done.18
  126.1 23.8 %collective-permute-done.3 = bf16[1024,448]{0,1:T(8,128)(2,1)S(1)} collective-permute-done((bf16[1024,448]{0,1:T(8,128)(2,1)S(1)}, bf16[1024,448]{0,1:T(8,128)(2,1)S(1)}, u32[]{:S(2)}, u32[]{:S(2)}) %collective-permute-start.3) | collective-permute-done | bytes 917536 | tf_op jit(solution)/shard_map/ppermute | solution.py:12
  149.9 0.9 copy-done.15
  150.8 0.8 fusion.44
  151.6 0.2 pad_maximum_fusion
  151.8 1.8 copy.17
  153.6 0.0 copy-start.9
  153.6 2.5 %reshape.20 = bf16[448,1344]{1,0:T(8,128)(2,1)} reshape(bf16[448,3,448]{2,1,0:T(4,128)(2,1)S(1)} %bitcast.120) | data formatting | bytes 2408448
  156.1 0.0 reduce-scatter.7.cloned.1.call-update
  156.2 0.0 copy-start.16
  156.2 0.6 fusion.69
  156.9 0.4 copy-done.1
  157.2 0.3 copy-done.16
  157.5 0.6 fusion.72
  158.2 0.5 copy-done.4
  158.7 0.1 copy-done.12
  158.8 0.5 copy-done.19
  159.3 2.7 %fusion.52 = bf16[1,1024,448]{1,2,0:T(8,128)(2,1)} fusion(f32[1024,448]{0,1:T(8,128)S(1)} %fusion.72, f32[1024,448]{0,1:T(8,128)S(1)} %fusion.69, bf16[1,1024,448]{1,2,0:T(8,128)(2,1)S(1)} %copy-done.4, bf16[1024,448]{0,1:T(8,128)(2,1)S(1)} %copy-done.14, bf16[1024,448]{0,1:T(8,128)(2,1)S(1)} %copy-done.19, bf16[1,448,448]{2,1,0:T(8,128)(2,1)S(1)} %copy-done.12), kind=kOutput, calls=%fused_computation.68 | convolution fusion | flops 422051840 | bytes 7741440 | tf_op jit(solution)/shard_map/dot_general | solution.py:27
  162.0 1.7 reshape.23
  163.7 0.3 copy.20
  164.0 15.7 %reduce-scatter.7.cloned.1.call-done = bf16[112,1344]{1,0:T(8,128)(2,1)} async-done(((bf16[448,1344]{1,0:T(8,128)(2,1)}), bf16[112,1344]{1,0:T(8,128)(2,1)}) %reduce-scatter.7.cloned.1.call-update) | async-done | bytes 301072
  179.8 1.7 reshape.21
  181.5 0.3 copy.18
  181.8 54.2 %all-reduce.2 = (f32[3,448,112]{2,1,0:T(8,128)}, f32[3,448,112]{2,1,0:T(8,128)}) all-reduce(bf16[3,448,112]{2,1,0:T(8,128)(2,1)S(1)} %copy.18, bf16[3,448,112]{2,1,0:T(8,128)(2,1)S(1)} %copy.20), channel_id=1, replica_groups=mesh['groups'=2,'seq'=4,'dp'=4] {'seq'}, use_global_device_ids=true, to_apply=%region_1.0 | all-reduce | flops 301056 | bytes 1806336 | tf_op jit(solution)/shard_map/psum | solution.py:82
  (34 shorter events, 0.1 us)
Async XLA Ops:
  7.2 4.5 %copy-start.2 = (bf16[1,1024,448]{1,2,0:T(8,128)(2,1)S(1)}, bf16[1,1024,448]{1,2,0:T(8,128)(2,1)}, u32[]{:S(2)}) copy-start(bf16[1,1024,448]{1,2,0:T(8,128)(2,1)} %param.4) | copy-start | bytes 2752516
  7.2 26.8 %all-gather.3.cloned.1.call-start = ((), (), s32[]{:S(2)}) async-start(), calls=%async_computation.2 | async-start | bytes 2293760 | tf_op jit(solution)/shard_map/all_gather | solution.py:38
  9.4 47.9 %all-gather.5.cloned.1.call-start = ((), (), s32[]{:S(2)}) async-start(), calls=%async_computation.3 | async-start | bytes 2293760 | tf_op jit(solution)/shard_map/all_gather | solution.py:56
  11.6 150.4 %reduce-scatter.9.cloned.1.call-start = ((), (), s32[]{:S(2)}) async-start(), calls=%async_computation.5 | async-start | bytes 1576960
  13.2 65.6 %collective-permute-start = (bf16[1024,448]{0,1:T(8,128)(2,1)}, bf16[1024,448]{0,1:T(8,128)(2,1)}, u32[]{:S(2)}, u32[]{:S(2)}) collective-permute-start(bf16[1024,448]{0,1:T(8,128)(2,1)} %fusion.26), channel_id=1, source_target_pairs={{0,8},{4,12},{1,9},{5,13},{2,10},{6,14},{3,11},{7,15},{16,24},{20,... | collective-permute-start | bytes 2752520 | tf_op jit(solution)/shard_map/ppermute | solution.py:12
  20.1 60.7 %collective-permute-start.1 = (bf16[1024,448]{0,1:T(8,128)(2,1)}, bf16[1024,448]{0,1:T(8,128)(2,1)}, u32[]{:S(2)}, u32[]{:S(2)}) collective-permute-start(bf16[1024,448]{0,1:T(8,128)(2,1)} %fusion.26), channel_id=1, source_target_pairs={{8,0},{12,4},{9,1},{13,5},{10,2},{14,6},{11,3},{15,7},{24,16},{28,... | collective-permute-start | bytes 2752520 | tf_op jit(solution)/shard_map/ppermute | solution.py:12
  21.4 63.8 %collective-permute-start.2 = (bf16[1024,448]{0,1:T(8,128)(2,1)}, bf16[1024,448]{0,1:T(8,128)(2,1)}, u32[]{:S(2)}, u32[]{:S(2)}) collective-permute-start(bf16[1024,448]{0,1:T(8,128)(2,1)} %bitcast), channel_id=1, source_target_pairs={} | collective-permute-start | bytes 2752520 | tf_op jit(solution)/shard_map/ppermute | solution.py:12
  66.0 12.8 %copy-start = (bf16[1,448,448]{2,1,0:T(8,128)(2,1)}, bf16[1,448,448]{2,1,0:T(8,128)(2,1)S(1)}, u32[]{:S(2)}) copy-start(bf16[1,448,448]{2,1,0:T(8,128)(2,1)S(1)} %copy.21) | copy-start | bytes 1204228
  68.0 5.4 %copy-start.6 = (bf16[1,448,448]{1,0,2:T(2,128)(2,1)S(1)}, bf16[1,448,448]{1,0,2:T(2,128)(2,1)}, u32[]{:S(2)}) copy-start(bf16[1,448,448]{1,0,2:T(2,128)(2,1)} %get-tuple-element.6) | copy-start | bytes 1204228
  69.9 4.8 %copy-start.8 = (bf16[1,448,448]{2,1,0:T(8,128)(2,1)S(1)}, bf16[1,448,448]{2,1,0:T(8,128)(2,1)}, u32[]{:S(2)}) copy-start(bf16[1,448,448]{2,1,0:T(8,128)(2,1)} %copy.22) | copy-start | bytes 1204228
  78.8 1.9 copy-start.11
  82.8 2.4 copy-start.17
  89.2 2.8 %copy-start.10 = (bf16[1,448,448]{2,1,0:T(8,128)(2,1)S(1)}, bf16[1,448,448]{2,1,0:T(8,128)(2,1)}, u32[]{:S(2)}) copy-start(bf16[1,448,448]{2,1,0:T(8,128)(2,1)} %copy.24) | copy-start | bytes 1204228
  91.7 3.4 %copy-start.5 = (bf16[1,448,448]{1,0,2:T(2,128)(2,1)S(1)}, bf16[1,448,448]{1,0,2:T(2,128)(2,1)}, u32[]{:S(2)}) copy-start(bf16[1,448,448]{1,0,2:T(2,128)(2,1)} %get-tuple-element.5) | copy-start | bytes 1204228
  91.7 4.8 %copy-start.7 = (f32[1024,448]{0,1:T(8,128)S(1)}, f32[1024,448]{0,1:T(8,128)}, u32[]{:S(2)}) copy-start(f32[1024,448]{0,1:T(8,128)} %fusion.57) | copy-start | bytes 5505028
  91.8 88.0 %reduce-scatter.7.cloned.1.call-start = ((), (), s32[]{:S(2)}) async-start(), calls=%async_computation.4 | async-start | bytes 1576960
  96.5 10.0 %copy-start.3 = (bf16[1,1024,448]{1,2,0:T(8,128)(2,1)S(1)}, bf16[1,1024,448]{1,2,0:T(8,128)(2,1)}, u32[]{:S(2)}) copy-start(bf16[1,1024,448]{1,2,0:T(8,128)(2,1)} %param.4) | copy-start | bytes 2752516
  100.7 6.7 %copy-start.13 = (bf16[1024,448]{0,1:T(8,128)(2,1)}, bf16[1024,448]{0,1:T(8,128)(2,1)S(1)}, u32[]{:S(2)}) copy-start(bf16[1024,448]{0,1:T(8,128)(2,1)S(1)} %fusion.17) | copy-start | bytes 2752516
  100.7 24.5 %collective-permute-start.4 = (bf16[1024,448]{0,1:T(8,128)(2,1)S(1)}, bf16[1024,448]{0,1:T(8,128)(2,1)S(1)}, u32[]{:S(2)}, u32[]{:S(2)}) collective-permute-start(bf16[1024,448]{0,1:T(8,128)(2,1)S(1)} %fusion.17), channel_id=1, source_target_pairs={{0,8},{4,12},{1,9},{5,13},{2,10},{6,14},{3,11},{7,15},{16,24},{20,... | collective-permute-start | bytes 2752520 | tf_op jit(solution)/shard_map/ppermute | solution.py:12
  105.2 44.7 %collective-permute-start.3 = (bf16[1024,448]{0,1:T(8,128)(2,1)S(1)}, bf16[1024,448]{0,1:T(8,128)(2,1)S(1)}, u32[]{:S(2)}, u32[]{:S(2)}) collective-permute-start(bf16[1024,448]{0,1:T(8,128)(2,1)S(1)} %fusion.17), channel_id=1, source_target_pairs={{8,0},{12,4},{9,1},{13,5},{10,2},{14,6},{11,3},{15,7},{24,16},{28,... | collective-permute-start | bytes 2752520 | tf_op jit(solution)/shard_map/ppermute | solution.py:12
  125.2 0.9 copy-start.18
  149.9 0.9 copy-start.15
  153.6 2.5 %copy-start.9 = (bf16[1,448,448]{2,1,0:T(8,128)(2,1)S(1)}, bf16[1,448,448]{2,1,0:T(8,128)(2,1)}, u32[]{:S(2)}) copy-start(bf16[1,448,448]{2,1,0:T(8,128)(2,1)} %copy.22) | copy-start | bytes 1204228
  153.6 2.5 %copy-start.14 = (bf16[1024,448]{0,1:T(8,128)(2,1)S(1)}, bf16[1024,448]{0,1:T(8,128)(2,1)}, u32[]{:S(2)}) copy-start(bf16[1024,448]{0,1:T(8,128)(2,1)} %copy-done.13) | copy-start | bytes 2752516
  156.2 1.0 copy-start.1
  156.2 1.3 copy-start.16
  157.5 1.2 copy-start.4
  157.5 1.3 copy-start.12
  157.5 1.8 copy-start.19
Sparse Core Ops, SparseCore 0:
  10.1 23.8 all-gather.2
  36.1 21.1 all-gather.4
  91.9 26.2 reduce-scatter.8
  156.3 23.4 reduce-scatter.6
where the time goes:
time: 243 us
  waiting for transfers between devices  85.6 us (35%)
  blocking collectives  54.2 us (22%)
  local copies, waits for them, and re-layouts  44.6 us (18%)
  matrix products  26.1 us (11%)
  starting transfers between devices  15.9 us (7%)
  between operations  14.1 us (6%)
    psum x1, blocking collectives, on_device(): lax.psum(lax.psum_scatter(part_one, 'dp', scatter_dimension=2, tiled=True...  54.2 us
    ppermute x5, waiting for transfers between devices, shifted(): return lax.ppermute(block, axis, route)  41.6 us
    unnamed x56, local copies, waits for them, and re-layouts  32.2 us
    all_gather x1, waiting for transfers between devices, on_device(): full_two = lax.all_gather(weight_two, 'dp', axis=2, tiled=True)  17.2 us
    unnamed x6, waiting for transfers between devices  15.8 us
    ppermute x5, starting transfers between devices, shifted(): return lax.ppermute(block, axis, route)  15.6 us
    dot_general x6, matrix products, back_product(): lax.dot_general(tap, weight, (((1,), (1,)), ((), ())), preferred_element_...  14.4 us
    all_gather x1, waiting for transfers between devices, on_device(): full_one = lax.all_gather(first_weight_matrix, 'dp', axis=2, tiled=True)  11 us
  transfers between devices with their start and end apart: 9, of which 5 were waited for; matrix products, arithmetic and copies ran while one was open for 24% of the time, Pallas kernels for 0%

commit v1 on v0

--- a/solution.py
+++ b/solution.py
@@ -1,9 +1,18 @@
+import functools
 import math
 
 import jax
 import jax.numpy as jnp
 from jax import lax
+from jax.experimental import pallas as pl
+from jax.experimental.pallas import tpu as pltpu
 from jax.sharding import PartitionSpec as P
+
+
+MESH = pl.DeviceIdType.MESH
+FIRST_SPACING = 2048
+SECOND_SPACING = 4096
+CHUNKS = 4
 
 
 def shifted(block, axis, distance):
@@ -29,7 +38,7 @@
     )
 
 
-def on_device(inputs, cotangent, first_weight_matrix, weight_two):
+def spread_plan(inputs, cotangent, first_weight_matrix, weight_two):
     chans = inputs.shape[2]
     rows = inputs.shape[0] * inputs.shape[1]
     factor = 1.0 / math.sqrt(
@@ -85,6 +94,300 @@
     return (input_grad.reshape(inputs.shape), grad_one, grad_two)
 
 
+def pack(left, right):
+    cut = right.shape[1] // 128 * 128
+    return jnp.concatenate([left, right[:, cut:], right[:, :cut]], axis=1)
+
+
+def unpack(both):
+    chans = both.shape[1] // 2
+    rest = chans % 128
+    right = jnp.concatenate([both[:, chans + rest :], both[:, chans : chans + rest]], axis=1)
+    return both[:, :chans], right
+
+
+def gelu_and_slope(value):
+    inner = math.sqrt(2.0 / math.pi)
+    square = value * value
+    bend = jnp.tanh(inner * value * (1.0 + 0.044715 * square))
+    half = 0.5 * (1.0 + bend)
+    slope = half + 0.5 * value * (1.0 - bend * bend) * (inner * (1.0 + 3.0 * 0.044715 * square))
+    return value * half, slope
+
+
+def forward(rows, weight_t):
+    return lax.dot_general(
+        rows, weight_t, (((1,), (1,)), ((), ())), preferred_element_type=jnp.float32
+    )
+
+
+def backward(rows, weight_t):
+    return jnp.dot(rows, weight_t, preferred_element_type=jnp.float32)
+
+
+def outer(left, right):
+    return lax.dot_general(
+        left, right, (((0,), (0,)), ((), ())), preferred_element_type=jnp.float32
+    )
+
+
+def pair_kernel(
+    factor,
+    x_ref, c_ref, w1_ref, w2_ref,
+    ig_ref, gr_ref,
+    sendb, xs, retb, retr, igs, wts, wt, terms,
+    s_core, r_core, s_chip, r_chip, acc, s_near, r_near, s_far, r_far, s_last, r_last,
+    xs_send, xs_recv, ret_send, ret_recv, w_send, w_recv, red_send, red_recv,
+):
+    f32, bf16 = jnp.float32, jnp.bfloat16
+    chans = x_ref.shape[1]
+    half = x_ref.shape[0] // 2
+    rows = half // CHUNKS
+    width = wts.shape[1]
+    z, d = lax.axis_index("seq"), lax.axis_index("dp")
+    role = z // 2
+    other = 1 - role
+    far = lax.rem(z + 2, 4)
+    parity = lax.rem(z, 2)
+    near = z + 1 - 2 * parity
+    core = lax.rem(d, 2)
+    chip = d // 2
+    sibling = d + 1 - 2 * core
+    across = lax.rem(d + 2, 4)
+
+    barrier = pltpu.get_barrier_semaphore()
+    for j in (1, 2, 3):
+        pl.semaphore_signal(
+            barrier, inc=1, device_id={"dp": lax.rem(d + j, 4)}, device_id_type=MESH
+        )
+    for peer in (near, far):
+        pl.semaphore_signal(barrier, inc=1, device_id={"seq": peer}, device_id_type=MESH)
+
+    def at_rows(start, size):
+        return pl.ds(pl.multiple_of(start, 16), size)
+
+    def move(ch):
+        piece = at_rows(ch * rows, rows)
+        return pltpu.make_async_remote_copy(
+            src_ref=sendb.at[piece],
+            dst_ref=xs.at[role, piece],
+            send_sem=xs_send.at[ch],
+            recv_sem=xs_recv.at[ch],
+            device_id={"seq": far},
+            device_id_type=MESH,
+        )
+
+    def give_back(ch):
+        piece = at_rows(ch * (rows // 2), rows // 2)
+        return pltpu.make_async_remote_copy(
+            src_ref=retb.at[piece],
+            dst_ref=retr.at[piece],
+            send_sem=ret_send.at[ch],
+            recv_sem=ret_recv.at[ch],
+            device_id={"seq": far},
+            device_id_type=MESH,
+        )
+
+    def pack_chunk(ch, carry):
+        from_rows = at_rows(other * half + ch * rows, rows)
+        sendb[at_rows(ch * rows, rows), :] = pack(x_ref[from_rows, :], c_ref[from_rows, :])
+        return carry
+
+    lax.fori_loop(0, CHUNKS, pack_chunk, 0)
+    pl.semaphore_wait(barrier, 5)
+    for ch in range(CHUNKS):
+        move(ch).start()
+
+    taps = (w1_ref.at[0], w1_ref.at[1], w1_ref.at[2], w2_ref.at[1])
+    mine = at_rows(d * width, width)
+    for k, tap in enumerate(taps):
+        turned = tap[...].astype(f32).T.astype(bf16)
+        wts[k] = turned
+        wt[k, mine, :] = turned
+
+    def share(j):
+        return pltpu.make_async_remote_copy(
+            src_ref=wts,
+            dst_ref=wt.at[:, mine],
+            send_sem=w_send.at[j - 1],
+            recv_sem=w_recv.at[j - 1],
+            device_id={"dp": lax.rem(d + j, 4)},
+            device_id_type=MESH,
+        )
+
+    for j in (1, 2, 3):
+        share(j).start()
+
+    def keep_chunk(ch, carry):
+        from_rows = at_rows(role * half + ch * rows, rows)
+        xs[role, at_rows(ch * rows, rows), :] = pack(x_ref[from_rows, :], c_ref[from_rows, :])
+        return carry
+
+    lax.fori_loop(0, CHUNKS, keep_chunk, 0)
+    terms[...] = jnp.zeros_like(terms)
+    for j in (1, 2, 3):
+        share(j).wait()
+
+    def work(ch, carry):
+        move(ch).wait_recv()
+
+        @pl.when(ch == CHUNKS - 1)
+        def _():
+            for early in range(CHUNKS - 1):
+                give_back(early).start()
+
+        piece = at_rows(ch * rows, rows)
+        both = xs[:, piece, :].reshape(2 * rows, 2 * chans)
+        x_b, c_b = unpack(both)
+        x_f = x_b.astype(f32)
+        act, slope_x = gelu_and_slope(x_f)
+        act = act.astype(bf16)
+        cross = jnp.concatenate([forward(act[rows:], wt[2]), forward(act[:rows], wt[0])], axis=0)
+        hidden = (x_f + (forward(act, wt[1]) + cross)).astype(bf16).astype(f32)
+        act_one, slope_h = gelu_and_slope(hidden)
+        act_one = act_one.astype(bf16)
+        grad_mid = (c_b.astype(f32) + slope_h * backward(c_b, wt[3])).astype(bf16)
+        cross = jnp.concatenate(
+            [backward(grad_mid[rows:], wt[0]), backward(grad_mid[:rows], wt[2])], axis=0
+        )
+        delta = backward(grad_mid, wt[1]) + cross
+        result = (grad_mid.astype(f32) + slope_x * delta).astype(bf16)
+        igs[...] = result.reshape(2, rows, chans)
+        terms[3] += outer(c_b, act_one)
+        terms[0] += outer(grad_mid[rows:], act[:rows])
+        terms[1] += outer(grad_mid, act)
+        terms[2] += outer(grad_mid[:rows], act[rows:])
+        ig_ref[at_rows(role * half + ch * rows, rows), :] = igs[role]
+        back = igs[other]
+        retb[at_rows(ch * (rows // 2), rows // 2), :] = pack(back[: rows // 2], back[rows // 2 :])
+        return carry
+
+    lax.fori_loop(0, CHUNKS, work, 0)
+    give_back(CHUNKS - 1).start()
+
+    def slice_of(owner):
+        owned = at_rows(owner * width, width)
+        own = [terms[k, owned, :] * factor for k in range(4)]
+        return pack(own[0], own[1]), pack(own[2], own[3])
+
+    def reduce_copy(index, src, dst, axis, peer):
+        return pltpu.make_async_remote_copy(
+            src_ref=src,
+            dst_ref=dst,
+            send_sem=red_send.at[index],
+            recv_sem=red_recv.at[index],
+            device_id={axis: peer},
+            device_id_type=MESH,
+        )
+
+    to_core = []
+    for j, for_chip in enumerate((1 - chip, chip)):
+        first, second = slice_of(2 * for_chip + 1 - core)
+        s_core[j, 0] = first.astype(bf16)
+        s_core[j, 1] = second.astype(bf16)
+        to_core.append(reduce_copy(j, s_core.at[j], r_core.at[j], "dp", sibling))
+        to_core[j].start()
+    to_core[0].wait_recv()
+    for p, part in enumerate(slice_of(2 * (1 - chip) + core)):
+        s_chip[p] = (part + r_core[0, p].astype(f32)).astype(bf16)
+    to_chip = reduce_copy(2, s_chip, r_chip, "dp", across)
+    to_chip.start()
+    to_core[1].wait_recv()
+    for p, part in enumerate(slice_of(d)):
+        acc[p] = part + r_core[1, p].astype(f32)
+    to_chip.wait_recv()
+    for p in range(2):
+        acc[p] += r_chip[p].astype(f32)
+
+    s_near[...] = acc[1 - parity].astype(bf16)
+    to_near = reduce_copy(3, s_near, r_near, "seq", near)
+    to_near.start()
+    to_near.wait_recv()
+    s_far[...] = (acc[parity] + r_near[...].astype(f32)).astype(bf16)
+    to_far = reduce_copy(4, s_far, r_far, "seq", far)
+    to_far.start()
+
+    for ch in range(CHUNKS):
+        give_back(ch).wait_recv()
+        left, right = unpack(retr[ch * (rows // 2) : (ch + 1) * (rows // 2), :])
+        at = other * half + ch * rows
+        ig_ref[at_rows(at, rows // 2), :] = left
+        ig_ref[at_rows(at + rows // 2, rows // 2), :] = right
+
+    to_far.wait_recv()
+    s_last[...] = (s_far[...].astype(f32) + r_far[...].astype(f32)).astype(bf16)
+    to_last = reduce_copy(5, s_last, r_last, "seq", near)
+    to_last.start()
+    gr_ref[parity] = s_last[...].astype(f32)
+    to_last.wait_recv()
+    gr_ref[1 - parity] = r_last[...].astype(f32)
+
+    for ch in range(CHUNKS):
+        move(ch).wait_send()
+        give_back(ch).wait_send()
+    for copy in (*to_core, to_chip, to_near, to_far, to_last):
+        copy.wait_send()
+
+
+def pair_plan(inputs, cotangent, first_weight_matrix, weight_two):
+    positions, chans = inputs.shape[1:]
+    width = first_weight_matrix.shape[2]
+    factor = 1.0 / math.sqrt(
+        lax.axis_size("dp") * positions * lax.axis_size("seq")
+    )
+    half = positions // 2
+    f32, bf16 = jnp.float32, jnp.bfloat16
+    vmem = pl.BlockSpec(memory_space=pltpu.VMEM)
+    dma = pltpu.SemaphoreType.DMA
+    packed = (width, 2 * chans)
+    result, sums = pl.pallas_call(
+        functools.partial(pair_kernel, factor),
+        out_shape=(
+            jax.ShapeDtypeStruct((positions, chans), bf16),
+            jax.ShapeDtypeStruct((2, *packed), f32),
+        ),
+        in_specs=[vmem] * 4,
+        out_specs=(vmem, vmem),
+        scratch_shapes=[
+            pltpu.VMEM((half, 2 * chans), bf16),
+            pltpu.VMEM((2, half, 2 * chans), bf16),
+            pltpu.VMEM((half // 2, 2 * chans), bf16),
+            pltpu.VMEM((half // 2, 2 * chans), bf16),
+            pltpu.VMEM((2, half // CHUNKS, chans), bf16),
+            pltpu.VMEM((4, width, chans), bf16),
+            pltpu.VMEM((4, chans, chans), bf16),
+            pltpu.VMEM((4, chans, chans), f32),
+            pltpu.VMEM((2, 2, *packed), bf16),
+            pltpu.VMEM((2, 2, *packed), bf16),
+            pltpu.VMEM((2, *packed), bf16),
+            pltpu.VMEM((2, *packed), bf16),
+            pltpu.VMEM((2, *packed), f32),
+            *[pltpu.VMEM(packed, bf16)] * 6,
+            dma((CHUNKS,)), dma((CHUNKS,)), dma((CHUNKS,)), dma((CHUNKS,)),
+            dma((3,)), dma((3,)), dma((6,)), dma((6,)),
+        ],
+        compiler_params=pltpu.CompilerParams(
+            collective_id=0, has_side_effects=True, vmem_limit_bytes=48 * 2**20
+        ),
+    )(inputs[0], cotangent[0], first_weight_matrix, weight_two)
+    pair_one = unpack(sums[0])
+    pair_two = unpack(sums[1])
+    grad_one = jnp.stack([pair_one[0].T, pair_one[1].T, pair_two[0].T])
+    middle = pair_two[1].T
+    outside = jnp.zeros_like(middle)
+    grad_two = jnp.stack([outside, middle, outside])
+    return result[None], grad_one, grad_two
+
+
+def on_device(inputs, cotangent, first_weight_matrix, weight_two):
+    sequences, positions, chans = inputs.shape
+    length = positions * lax.axis_size("seq")
+    paired = lax.axis_size("seq") == 4 and lax.axis_size("dp") == 4 and sequences == 1
+    if paired and length == 2 * FIRST_SPACING and length <= SECOND_SPACING:
+        return pair_plan(inputs, cotangent, first_weight_matrix, weight_two)
+    return spread_plan(inputs, cotangent, first_weight_matrix, weight_two)
+
+
 def solution(mesh):
     placed = (
         P(("groups", "dp"), "seq", None),

time: 243 us -> 90.2 us (0.37)
  waiting for transfers between devices: 85.6 us -> 0 us
  Pallas kernels: 0 us -> 81.8 us
  blocking collectives: 54.2 us -> 0 us
  local copies, waits for them, and re-layouts: 44.6 us -> 7.28 us
  matrix products: 26.1 us -> 0 us
  starting transfers between devices: 15.9 us -> 0 us
  between operations: 14.1 us -> 0.75 us
    pallas_call x0 -> x1, Pallas kernels: none -> 81.8 us  [pair_plan(): pl.pallas_call(functools.partial(pair_kernel, factor), out_shape=(jax.Sha...]
    psum x1 -> x0, blocking collectives: 54.2 us -> none  [on_device(): lax.psum(lax.psum_scatter(part_one, 'dp', scatter_dimension=2, tiled=True...]
    ppermute x5 -> x0, waiting for transfers between devices: 41.6 us -> none  [shifted(): return lax.ppermute(block, axis, route)]
    all_gather x2 -> x0, waiting for transfers between devices: 28.2 us -> none  [the longest x1 17.2 us: on_device(): full_two = lax.all_gather(weight_two, 'dp', axis=2, tiled=True)]
    dot_general x14 -> x0, matrix products: 26.1 us -> none  [the longest x6 14.4 us: back_product(): lax.dot_general(tap, weight, (((1,), (1,)), ((), ())), preferred_element_...]
    unnamed x56 -> x11, local copies, waits for them, and re-layouts: 32.2 us -> 6.98 us
    unnamed x6 -> x0, waiting for transfers between devices: 15.8 us -> none
    ppermute x5 -> x0, starting transfers between devices: 15.6 us -> none  [shifted(): return lax.ppermute(block, axis, route)]
  transfers between devices with their start and end apart: 9 -> 0, of which waited for: 5 -> 0; matrix products, arithmetic and copies ran while one was open for 24% -> 0% of each run, Pallas kernels for 0% -> 0%
where the time goes in v1:
time: 90.2 us; the launch traced here: 90 us
  Pallas kernels  81.8 us (91%)
  local copies, waits for them, and re-layouts  7.28 us (8%)
    pallas_call x1, Pallas kernels, pair_plan(): pl.pallas_call(functools.partial(pair_kernel, factor), out_shape=(jax.Sha...  81.8 us
    unnamed x11, local copies, waits for them, and re-layouts  6.98 us

profile of v1, /device:TPU:0, one launch (start us, length us, event | category | flops | bytes accessed | tf_op | source)
XLA Modules:
  0.0 90.0 jit_solution(14905351450196200959)
XLA Ops:
  0.6 0.0 copy-start.2
  0.6 1.5 %copy.7 = bf16[1,1024,448]{2,1,0:T(8,128)(2,1)S(1)} copy(bf16[1,1024,448]{1,2,0:T(8,128)(2,1)} %param.4) | data formatting | bytes 1835008 | tf_op args[0]
  2.2 0.0 copy-done.2
  2.2 0.0 copy-start
  2.2 0.5 copy.8
  2.7 0.4 copy-done
  3.2 0.0 copy-start.1
  3.2 1.0 %copy-done.1 = bf16[3,448,112]{2,1,0:T(8,128)(2,1)S(1)} copy-done((bf16[3,448,112]{2,1,0:T(8,128)(2,1)S(1)}, bf16[3,448,112]{2,1,0:T(8,128)(2,1)}, u32[]{:S(2)}) %copy-start.1) | copy-done | bytes 301080
  4.2 81.8 %shard_map.67 = (bf16[1024,448]{1,0:T(8,128)(2,1)S(1)}, f32[2,112,896]{2,1,0:T(8,128)S(1)}) custom-call(bf16[1024,448]{1,0:T(8,128)(2,1)S(1)} %bitcast.23, bf16[1024,448]{1,0:T(8,128)(2,1)S(1)} %bitcast.24, bf16[3,448,112]{2,1,0:T(8,128)(2,1)S(1)} %copy-done, bf16[3,448,112]{2,1,0:T(8,128)(2,1)S(1)} %copy-done.1), custom_call_target="tpu_custom_call" | custom-call | tf_op jit(solution)/shard_map/pallas_call | solution.py:343
  86.0 0.1 slice_bitcast_fusion.1
  86.1 0.1 slice.34
  86.3 1.1 %copy.10 = f32[3,448,112]{2,1,0:T(8,128)} copy(f32[3,448,112]{1,2,0:T(8,128)S(1)} %pad_maximum_fusion) | data formatting | bytes 1204224
  87.4 0.1 slice.37
  87.5 0.1 pad_maximum_fusion.1
  87.6 1.1 %copy.11 = f32[3,448,112]{2,1,0:T(8,128)} copy(f32[3,448,112]{1,2,0:T(8,128)S(1)} %pad_maximum_fusion.1) | data formatting | bytes 1204224
  88.7 1.3 %copy.9 = bf16[1,1024,448]{1,2,0:T(8,128)(2,1)} copy(bf16[1,1024,448]{2,1,0:T(8,128)(2,1)S(1)} %bitcast.25) | data formatting | bytes 1835008
  (7 shorter events, 0.2 us)
Async XLA Ops:
  0.6 1.6 %copy-start.2 = (bf16[1,1024,448]{1,2,0:T(8,128)(2,1)S(1)}, bf16[1,1024,448]{1,2,0:T(8,128)(2,1)}, u32[]{:S(2)}) copy-start(bf16[1,1024,448]{1,2,0:T(8,128)(2,1)} %param.5) | copy-start | bytes 2752516
  2.2 1.0 %copy-start = (bf16[3,448,112]{2,1,0:T(8,128)(2,1)S(1)}, bf16[3,448,112]{2,1,0:T(8,128)(2,1)}, u32[]{:S(2)}) copy-start(bf16[3,448,112]{2,1,0:T(8,128)(2,1)} %w1_ref.1) | copy-start | bytes 903172
  3.2 1.0 %copy-start.1 = (bf16[3,448,112]{2,1,0:T(8,128)(2,1)S(1)}, bf16[3,448,112]{2,1,0:T(8,128)(2,1)}, u32[]{:S(2)}) copy-start(bf16[3,448,112]{2,1,0:T(8,128)(2,1)} %w2_ref.1) | copy-start | bytes 903172

commit v2 on v0

--- a/solution.py
+++ b/solution.py
@@ -1,9 +1,19 @@
+import functools
 import math
 
 import jax
 import jax.numpy as jnp
 from jax import lax
+from jax.experimental import pallas as pl
+from jax.experimental.pallas import tpu as pltpu
 from jax.sharding import PartitionSpec as P
+
+
+MESH = pl.DeviceIdType.MESH
+FIRST_SPACING = 2048
+SECOND_SPACING = 4096
+CHUNKS = 4
+AHEAD = 2
 
 
 def shifted(block, axis, distance):
@@ -29,7 +39,7 @@
     )
 
 
-def on_device(inputs, cotangent, first_weight_matrix, weight_two):
+def spread_plan(inputs, cotangent, first_weight_matrix, weight_two):
     chans = inputs.shape[2]
     rows = inputs.shape[0] * inputs.shape[1]
     factor = 1.0 / math.sqrt(
@@ -85,6 +95,310 @@
     return (input_grad.reshape(inputs.shape), grad_one, grad_two)
 
 
+def pack(left, right):
+    cut = right.shape[1] // 128 * 128
+    return jnp.concatenate([left, right[:, cut:], right[:, :cut]], axis=1)
+
+
+def unpack(both):
+    chans = both.shape[1] // 2
+    rest = chans % 128
+    right = jnp.concatenate([both[:, chans + rest :], both[:, chans : chans + rest]], axis=1)
+    return both[:, :chans], right
+
+
+def gelu_and_slope(value):
+    inner = math.sqrt(2.0 / math.pi)
+    square = value * value
+    bend = jnp.tanh(inner * value * (1.0 + 0.044715 * square))
+    half = 0.5 * (1.0 + bend)
+    slope = half + 0.5 * value * (1.0 - bend * bend) * (inner * (1.0 + 3.0 * 0.044715 * square))
+    return value * half, slope
+
+
+def product(left, right):
+    return jnp.dot(left, right, preferred_element_type=jnp.float32)
+
+
+def outer(left, right):
+    return lax.dot_general(
+        left, right, (((1,), (1,)), ((), ())), preferred_element_type=jnp.float32
+    )
+
+
+def pair_kernel(
+    factor,
+    x_ref, c_ref, w1_ref, w2_ref,
+    ig_ref, gr_ref,
+    xs, retb, igs, taps, wts, wt, wn, terms,
+    s_core, r_core, s_chip, r_chip, acc, s_near, r_near, s_far, r_far, s_last, r_last,
+    xs_send, xs_recv, own_sem, tap_sem, ret_send, ret_recv, w_send, w_recv, red_send, red_recv,
+):
+    f32, bf16 = jnp.float32, jnp.bfloat16
+    chans, positions = x_ref.shape
+    half = positions // 2
+    size = half // CHUNKS
+    width = wts.shape[1]
+    z, d = lax.axis_index("seq"), lax.axis_index("dp")
+    role = z // 2
+    other = 1 - role
+    far = lax.rem(z + 2, 4)
+    parity = lax.rem(z, 2)
+    near = z + 1 - 2 * parity
+    core = lax.rem(d, 2)
+    chip = d // 2
+    sibling = d + 1 - 2 * core
+    across = lax.rem(d + 2, 4)
+
+    barrier = pltpu.get_barrier_semaphore()
+    for axis, peer in (("seq", far), ("seq", near), ("dp", sibling), ("dp", across)):
+        pl.semaphore_signal(barrier, inc=1, device_id={axis: peer}, device_id_type=MESH)
+
+    own_half = pl.ds(pl.multiple_of(role * half, 128), half)
+    own_copies = [
+        pltpu.make_async_copy(ref.at[:, own_half], xs.at[role, i], own_sem.at[i])
+        for i, ref in enumerate((x_ref, c_ref))
+    ]
+    tap_copies = [
+        pltpu.make_async_copy(w1_ref, taps.at[pl.ds(0, 3)], tap_sem.at[0]),
+        pltpu.make_async_copy(w2_ref.at[1], taps.at[3], tap_sem.at[1]),
+    ]
+
+    def columns(start, count):
+        return pl.ds(pl.multiple_of(start, 128), count)
+
+    def owned_rows(owner):
+        return pl.ds(pl.multiple_of(owner * width, 16), width)
+
+    def remote(src, dst, send, recv, axis, peer):
+        return pltpu.make_async_remote_copy(
+            src_ref=src, dst_ref=dst, send_sem=send, recv_sem=recv,
+            device_id={axis: peer}, device_id_type=MESH,
+        )
+
+    def move(ch):
+        return [
+            remote(
+                ref.at[:, columns(other * half + ch * size, size)],
+                xs.at[role, i, :, columns(ch * size, size)],
+                xs_send.at[ch, i], xs_recv.at[ch, i], "seq", far,
+            )
+            for i, ref in enumerate((x_ref, c_ref))
+        ]
+
+    def give_back(ch):
+        return remote(
+            retb.at[:, columns(ch * size, size)],
+            ig_ref.at[:, columns(role * half + ch * size, size)],
+            ret_send.at[ch], ret_recv.at[ch], "seq", far,
+        )
+
+    for copy in tap_copies:
+        copy.start()
+    pl.semaphore_wait(barrier, 4)
+    for ch in range(AHEAD):
+        for copy in move(ch):
+            copy.start()
+    for copy in own_copies:
+        copy.start()
+
+    for copy in tap_copies:
+        copy.wait()
+    for k in range(4):
+        turned = taps[k].astype(f32).T.astype(bf16)
+        wts[k] = turned
+        wt[k, owned_rows(d), :] = turned
+    shares = [
+        remote(
+            wts, wt.at[:, owned_rows(d)], w_send.at[j], w_recv.at[j], "dp", peer
+        )
+        for j, peer in enumerate((across, sibling))
+    ]
+    for copy in shares:
+        copy.start()
+    terms[...] = jnp.zeros_like(terms)
+    shares[0].wait_recv()
+    arrived = wt.at[:, owned_rows(across)]
+    passed = remote(arrived, arrived, w_send.at[2], w_recv.at[2], "dp", sibling)
+    passed.start()
+    shares[1].wait_recv()
+    passed.wait_recv()
+    for k in range(4):
+        wn[k] = wt[k].astype(f32).T.astype(bf16)
+    for copy in own_copies:
+        copy.wait()
+
+    def work(ch, carry):
+        for copy in move(ch):
+            copy.wait_recv()
+
+        @pl.when(ch + AHEAD < CHUNKS)
+        def _():
+            for copy in move(ch + AHEAD):
+                copy.start()
+
+        @pl.when(ch == CHUNKS - 1)
+        def _():
+            for early in range(CHUNKS - 1):
+                give_back(early).start()
+
+        piece = columns(ch * size, size)
+        x_f = jnp.concatenate([xs[0, 0, :, piece], xs[1, 0, :, piece]], axis=1).astype(f32)
+        c_b = jnp.concatenate([xs[0, 1, :, piece], xs[1, 1, :, piece]], axis=1)
+        act, slope_x = gelu_and_slope(x_f)
+        act = act.astype(bf16)
+        low, high = act[:, :size], act[:, size:]
+        cross = jnp.concatenate([product(wt[2], high), product(wt[0], low)], axis=1)
+        hidden = (x_f + (product(wt[1], act) + cross)).astype(bf16).astype(f32)
+        act_one, slope_h = gelu_and_slope(hidden)
+        act_one = act_one.astype(bf16)
+        grad_mid = (c_b.astype(f32) + slope_h * product(wn[3], c_b)).astype(bf16)
+        g_low, g_high = grad_mid[:, :size], grad_mid[:, size:]
+        terms[3] += outer(c_b, act_one)
+        terms[0] += outer(g_high, low)
+        terms[1] += outer(grad_mid, act)
+        terms[2] += outer(g_low, high)
+        cross = jnp.concatenate([product(wn[0], g_high), product(wn[2], g_low)], axis=1)
+        delta = product(wn[1], grad_mid) + cross
+        result = (grad_mid.astype(f32) + slope_x * delta).astype(bf16)
+        igs[0] = result[:, :size]
+        igs[1] = result[:, size:]
+        ig_ref[:, columns(role * half + ch * size, size)] = igs[role]
+        retb[:, piece] = igs[other]
+        return carry
+
+    lax.fori_loop(0, CHUNKS, work, 0)
+    give_back(CHUNKS - 1).start()
+
+    steps = [(0, 48), (48, 32), (80, 32)] if width == 112 else [(0, width)]
+
+    def slice_of(owner, start, count):
+        owned = pl.ds(pl.multiple_of(owner * width + start, 16), count)
+        own = [terms[k, owned, :] * factor for k in range(4)]
+        return pack(own[0], own[1]), pack(own[2], own[3])
+
+    def reduce_copy(kind, q, src, dst, axis, peer):
+        return remote(src, dst, red_send.at[kind, q], red_recv.at[kind, q], axis, peer)
+
+    copies = [[], [], [], [], [], []]
+    for j, for_chip in enumerate((1 - chip, chip)):
+        for q, (start, count) in enumerate(steps):
+            span = pl.ds(start, count)
+            for p, part in enumerate(slice_of(2 * for_chip + 1 - core, start, count)):
+                s_core[j, p, span, :] = part.astype(bf16)
+            copies[j].append(
+                reduce_copy(
+                    j, q, s_core.at[j, :, span], r_core.at[j, :, span], "dp", sibling
+                )
+            )
+            copies[j][q].start()
+    for q, (start, count) in enumerate(steps):
+        span = pl.ds(start, count)
+        copies[0][q].wait_recv()
+        for p, part in enumerate(slice_of(2 * (1 - chip) + core, start, count)):
+            s_chip[p, span, :] = (part + r_core[0, p, span, :].astype(f32)).astype(bf16)
+        copies[2].append(
+            reduce_copy(2, q, s_chip.at[:, span], r_chip.at[:, span], "dp", across)
+        )
+        copies[2][q].start()
+    for q, (start, count) in enumerate(steps):
+        span = pl.ds(start, count)
+        copies[1][q].wait_recv()
+        for p, part in enumerate(slice_of(d, start, count)):
+            acc[p, span, :] = part + r_core[1, p, span, :].astype(f32)
+    for q, (start, count) in enumerate(steps):
+        span = pl.ds(start, count)
+        copies[2][q].wait_recv()
+        for p in range(2):
+            acc[p, span, :] += r_chip[p, span, :].astype(f32)
+        s_near[span, :] = acc[1 - parity, span, :].astype(bf16)
+        copies[3].append(reduce_copy(3, q, s_near.at[span], r_near.at[span], "seq", near))
+        copies[3][q].start()
+    for q, (start, count) in enumerate(steps):
+        span = pl.ds(start, count)
+        copies[3][q].wait_recv()
+        s_far[span, :] = (acc[parity, span, :] + r_near[span, :].astype(f32)).astype(bf16)
+        copies[4].append(reduce_copy(4, q, s_far.at[span], r_far.at[span], "seq", far))
+        copies[4][q].start()
+    for q, (start, count) in enumerate(steps):
+        span = pl.ds(start, count)
+        copies[4][q].wait_recv()
+        total = (s_far[span, :].astype(f32) + r_far[span, :].astype(f32)).astype(bf16)
+        s_last[span, :] = total
+        copies[5].append(reduce_copy(5, q, s_last.at[span], r_last.at[span], "seq", near))
+        copies[5][q].start()
+        for i, part in enumerate(unpack(total.astype(f32))):
+            gr_ref[2 * parity + i, span, :] = part
+    for q, (start, count) in enumerate(steps):
+        span = pl.ds(start, count)
+        copies[5][q].wait_recv()
+        for i, part in enumerate(unpack(r_last[span, :].astype(f32))):
+            gr_ref[2 * (1 - parity) + i, span, :] = part
+
+    for ch in range(CHUNKS):
+        give_back(ch).wait()
+        for copy in move(ch):
+            copy.wait_send()
+    for group in (shares, [passed], *copies):
+        for copy in group:
+            copy.wait_send()
+
+
+def pair_plan(inputs, cotangent, first_weight_matrix, weight_two):
+    positions, chans = inputs.shape[1:]
+    width = first_weight_matrix.shape[2]
+    factor = 1.0 / math.sqrt(
+        lax.axis_size("dp") * positions * lax.axis_size("seq")
+    )
+    half = positions // 2
+    f32, bf16 = jnp.float32, jnp.bfloat16
+    vmem = pl.BlockSpec(memory_space=pltpu.VMEM)
+    hbm = pl.BlockSpec(memory_space=pltpu.HBM)
+    dma = pltpu.SemaphoreType.DMA
+    packed = (width, 2 * chans)
+    result, sums = pl.pallas_call(
+        functools.partial(pair_kernel, factor),
+        out_shape=(
+            jax.ShapeDtypeStruct((chans, positions), bf16),
+            jax.ShapeDtypeStruct((4, width, chans), f32),
+        ),
+        in_specs=[hbm] * 4,
+        out_specs=(vmem, vmem),
+        scratch_shapes=[
+            pltpu.VMEM((2, 2, chans, half), bf16),
+            pltpu.VMEM((chans, half), bf16),
+            pltpu.VMEM((2, chans, half // CHUNKS), bf16),
+            pltpu.VMEM((4, chans, width), bf16),
+            pltpu.VMEM((4, width, chans), bf16),
+            pltpu.VMEM((4, chans, chans), bf16),
+            pltpu.VMEM((4, chans, chans), bf16),
+            pltpu.VMEM((4, chans, chans), f32),
+            pltpu.VMEM((2, 2, *packed), bf16),
+            pltpu.VMEM((2, 2, *packed), bf16),
+            pltpu.VMEM((2, *packed), bf16),
+            pltpu.VMEM((2, *packed), bf16),
+            pltpu.VMEM((2, *packed), f32),
+            *[pltpu.VMEM(packed, bf16)] * 6,
+            dma((CHUNKS, 2)), dma((CHUNKS, 2)), dma((2,)), dma((2,)),
+            dma((CHUNKS,)), dma((CHUNKS,)), dma((3,)), dma((3,)), dma((6, 3)), dma((6, 3)),
+        ],
+        compiler_params=pltpu.CompilerParams(
+            collective_id=0, has_side_effects=True, vmem_limit_bytes=62 * 2**20
+        ),
+    )(inputs[0].T, cotangent[0].T, first_weight_matrix, weight_two)
+    sums = sums.transpose(0, 2, 1)
+    return result.T[None], sums[:3], jnp.pad(sums[3:], ((1, 1), (0, 0), (0, 0)))
+
+
+def on_device(inputs, cotangent, first_weight_matrix, weight_two):
+    sequences, positions, chans = inputs.shape
+    length = positions * lax.axis_size("seq")
+    paired = lax.axis_size("seq") == 4 and lax.axis_size("dp") == 4 and sequences == 1
+    if paired and length == 2 * FIRST_SPACING and length <= SECOND_SPACING:
+        return pair_plan(inputs, cotangent, first_weight_matrix, weight_two)
+    return spread_plan(inputs, cotangent, first_weight_matrix, weight_two)
+
+
 def solution(mesh):
     placed = (
         P(("groups", "dp"), "seq", None),

time: 243 us -> 85.3 us (0.35)
  waiting for transfers between devices: 85.6 us -> 0 us
  Pallas kernels: 0 us -> 78.9 us
  blocking collectives: 54.2 us -> 0 us
  local copies, waits for them, and re-layouts: 44.6 us -> 5.5 us
  matrix products: 26.1 us -> 0 us
  starting transfers between devices: 15.9 us -> 0 us
  between operations: 14.1 us -> 0.66 us
    pallas_call x0 -> x1, Pallas kernels: none -> 78.9 us  [pair_plan(): pl.pallas_call(functools.partial(pair_kernel, factor), out_shape=(jax.Sha...]
    psum x1 -> x0, blocking collectives: 54.2 us -> none  [on_device(): lax.psum(lax.psum_scatter(part_one, 'dp', scatter_dimension=2, tiled=True...]
    ppermute x5 -> x0, waiting for transfers between devices: 41.6 us -> none  [shifted(): return lax.ppermute(block, axis, route)]
    unnamed x56 -> x5, local copies, waits for them, and re-layouts: 32.2 us -> 2.5 us
    all_gather x2 -> x0, waiting for transfers between devices: 28.2 us -> none  [the longest x1 17.2 us: on_device(): full_two = lax.all_gather(weight_two, 'dp', axis=2, tiled=True)]
    dot_general x14 -> x0, matrix products: 26.1 us -> none  [the longest x6 14.4 us: back_product(): lax.dot_general(tap, weight, (((1,), (1,)), ((), ())), preferred_element_...]
    unnamed x6 -> x0, waiting for transfers between devices: 15.8 us -> none
    ppermute x5 -> x0, starting transfers between devices: 15.6 us -> none  [shifted(): return lax.ppermute(block, axis, route)]
  transfers between devices with their start and end apart: 9 -> 0, of which waited for: 5 -> 0; matrix products, arithmetic and copies ran while one was open for 24% -> 0% of each run, Pallas kernels for 0% -> 0%
where the time goes in v2:
time: 85.3 us; the launch traced here: 85.1 us
  Pallas kernels  78.9 us (92%)
  local copies, waits for them, and re-layouts  5.5 us (6%)
    pallas_call x1, Pallas kernels, pair_plan(): pl.pallas_call(functools.partial(pair_kernel, factor), out_shape=(jax.Sha...  78.9 us
    unnamed x5, local copies, waits for them, and re-layouts  2.5 us

profile of v2, /device:TPU:0, one launch (start us, length us, event | category | flops | bytes accessed | tf_op | source)
XLA Modules:
  0.0 85.1 jit_solution(12375612426592530922)
XLA Ops:
  0.6 78.9 %shard_map.67 = (bf16[448,1024]{1,0:T(8,128)(2,1)}, f32[4,112,448]{2,1,0:T(8,128)}) custom-call(bf16[448,1024]{1,0:T(8,128)(2,1)} %bitcast.13, bf16[448,1024]{1,0:T(8,128)(2,1)} %bitcast.14, bf16[3,448,112]{2,1,0:T(8,128)(2,1)} %w1_ref.1, bf16[3,448,112]{2,1,0:T(8,128)(2,1)} %w2_ref.1), custom_call_target="tpu_custom_call" | custom-call | tf_op jit(solution)/shard_map/pallas_call | solution.py:359
  79.6 1.0 %slice.9 = f32[1,448,112]{1,2,0:T(8,128)S(1)} slice(f32[4,448,112]{1,2,0:T(8,128)} %bitcast.11), slice={[3:4], [0:448], [0:112]} | slice | bytes 401408 | tf_op jit(solution)/shard_map/slice | solution.py:390
  80.5 1.1 %slice.8 = f32[3,448,112]{1,2,0:T(8,128)S(1)} slice(f32[4,448,112]{1,2,0:T(8,128)} %bitcast.12), slice={[0:3], [0:448], [0:112]} | slice | bytes 1204224 | tf_op jit(solution)/shard_map/slice | solution.py:390
  81.7 1.1 %copy.7 = f32[3,448,112]{2,1,0:T(8,128)} copy(f32[3,448,112]{1,2,0:T(8,128)S(1)} %slice.8) | data formatting | bytes 1204224
  82.8 0.0 copy-start
  82.8 0.1 copy.9
  82.9 0.9 %pad.4.clone = f32[3,448,112]{2,1,0:T(8,128)} pad(f32[1,448,112]{2,1,0:T(8,128)S(1)} %copy.9, f32[]{:T(128)} %constant.2.clone.1), padding=1_1x0_0x0_0 | pad | bytes 802820 | tf_op jit(solution)/shard_map/jit(_pad)/pad | solution.py:390
  83.8 0.3 copy-done
  84.2 0.9 %copy.11 = bf16[1,1024,448]{1,2,0:T(8,128)(2,1)} copy(bf16[1,1024,448]{1,2,0:T(8,128)(2,1)S(1)} %bitcast.10) | data formatting | bytes 1835008
Async XLA Ops:
  82.8 1.4 %copy-start = (bf16[448,1024]{1,0:T(8,128)(2,1)S(1)}, bf16[448,1024]{1,0:T(8,128)(2,1)}, u32[]{:S(2)}) copy-start(bf16[448,1024]{1,0:T(8,128)(2,1)} %get-tuple-element.5) | copy-start | bytes 2752516

commit v3 on v2

--- a/solution.py
+++ b/solution.py
@@ -129,8 +129,8 @@
 def pair_kernel(
     factor,
     x_ref, c_ref, w1_ref, w2_ref,
-    ig_ref, gr_ref,
-    xs, retb, igs, taps, wts, wt, wn, terms,
+    ig_ref, g_one_ref, g_two_ref,
+    sums, xs, retb, igs, taps, wts, wt, wn, terms,
     s_core, r_core, s_chip, r_chip, acc, s_near, r_near, s_far, r_far, s_last, r_last,
     xs_send, xs_recv, own_sem, tap_sem, ret_send, ret_recv, w_send, w_recv, red_send, red_recv,
 ):
@@ -268,7 +268,6 @@
         return carry
 
     lax.fori_loop(0, CHUNKS, work, 0)
-    give_back(CHUNKS - 1).start()
 
     steps = [(0, 48), (48, 32), (80, 32)] if width == 112 else [(0, width)]
 
@@ -320,6 +319,10 @@
         s_far[span, :] = (acc[parity, span, :] + r_near[span, :].astype(f32)).astype(bf16)
         copies[4].append(reduce_copy(4, q, s_far.at[span], r_far.at[span], "seq", far))
         copies[4][q].start()
+    give_back(CHUNKS - 1).start()
+    outside = jnp.zeros((width, chans), f32)
+    g_two_ref[0] = outside
+    g_two_ref[2] = outside
     for q, (start, count) in enumerate(steps):
         span = pl.ds(start, count)
         copies[4][q].wait_recv()
@@ -328,12 +331,15 @@
         copies[5].append(reduce_copy(5, q, s_last.at[span], r_last.at[span], "seq", near))
         copies[5][q].start()
         for i, part in enumerate(unpack(total.astype(f32))):
-            gr_ref[2 * parity + i, span, :] = part
+            sums[2 * parity + i, span, :] = part
     for q, (start, count) in enumerate(steps):
         span = pl.ds(start, count)
         copies[5][q].wait_recv()
         for i, part in enumerate(unpack(r_last[span, :].astype(f32))):
-            gr_ref[2 * (1 - parity) + i, span, :] = part
+            sums[2 * (1 - parity) + i, span, :] = part
+        for k in range(3):
+            g_one_ref[k, span, :] = sums[k, span, :]
+        g_two_ref[1, span, :] = sums[3, span, :]
 
     for ch in range(CHUNKS):
         give_back(ch).wait()
@@ -356,15 +362,17 @@
     hbm = pl.BlockSpec(memory_space=pltpu.HBM)
     dma = pltpu.SemaphoreType.DMA
     packed = (width, 2 * chans)
-    result, sums = pl.pallas_call(
+    result, grad_one, grad_two = pl.pallas_call(
         functools.partial(pair_kernel, factor),
         out_shape=(
             jax.ShapeDtypeStruct((chans, positions), bf16),
-            jax.ShapeDtypeStruct((4, width, chans), f32),
+            jax.ShapeDtypeStruct((3, width, chans), f32),
+            jax.ShapeDtypeStruct((3, width, chans), f32),
         ),
         in_specs=[hbm] * 4,
-        out_specs=(vmem, vmem),
+        out_specs=(vmem, vmem, vmem),
         scratch_shapes=[
+            pltpu.VMEM((4, width, chans), f32),
             pltpu.VMEM((2, 2, chans, half), bf16),
             pltpu.VMEM((chans, half), bf16),
             pltpu.VMEM((2, chans, half // CHUNKS), bf16),
@@ -386,8 +394,7 @@
             collective_id=0, has_side_effects=True, vmem_limit_bytes=62 * 2**20
         ),
     )(inputs[0].T, cotangent[0].T, first_weight_matrix, weight_two)
-    sums = sums.transpose(0, 2, 1)
-    return result.T[None], sums[:3], jnp.pad(sums[3:], ((1, 1), (0, 0), (0, 0)))
+    return result.T[None], grad_one.transpose(0, 2, 1), grad_two.transpose(0, 2, 1)
 
 
 def on_device(inputs, cotangent, first_weight_matrix, weight_two):

time: 85.3 us -> 83.1 us (0.974)
  local copies, waits for them, and re-layouts: 5.5 us -> 4.39 us
  Pallas kernels: 78.9 us -> 77.9 us
    slice x2 -> x0, local copies, waits for them, and re-layouts: 2.1 us -> none  [the longest x1 1.14 us: pair_plan(): sums[:3]]
    unnamed x5 -> x7, local copies, waits for them, and re-layouts: 2.5 us -> 4.39 us
    pallas_call x1, Pallas kernels: 78.9 us -> 77.9 us  [pair_plan(): pl.pallas_call(functools.partial(pair_kernel, factor), out_shape=(jax.Sha...]
    pad x1 -> x0, local copies, waits for them, and re-layouts: 0.9 us -> none  [pair_plan(): jnp.pad(sums[3:], ((1, 1), (0, 0), (0, 0)))]
where the time goes in v3:
time: 83.1 us; the launch traced here: 82.9 us
  Pallas kernels  77.9 us (94%)
  local copies, waits for them, and re-layouts  4.39 us (5%)
    pallas_call x1, Pallas kernels, pair_plan(): pl.pallas_call(functools.partial(pair_kernel, factor), out_shape=(jax.Sha...  77.9 us
    unnamed x7, local copies, waits for them, and re-layouts  4.39 us

profile of v3, /device:TPU:0, one launch (start us, length us, event | category | flops | bytes accessed | tf_op | source)
XLA Modules:
  0.0 82.9 jit_solution(17349782472840781453)
XLA Ops:
  0.6 77.9 %shard_map.67 = (bf16[448,1024]{1,0:T(8,128)(2,1)}, f32[3,112,448]{2,1,0:T(8,128)}, f32[3,112,448]{2,1,0:T(8,128)}) custom-call(bf16[448,1024]{1,0:T(8,128)(2,1)} %bitcast.12, bf16[448,1024]{1,0:T(8,128)(2,1)} %bitcast.13, bf16[3,448,112]{2,1,0:T(8,128)(2,1)} %w1_ref.1, bf16[3,448,112]{2,1,0:T(8,128)(2,1)} %w2_ref.1), custom_call_target="tpu_custom_call" | custom-call | tf_op jit(solution)/shard_map/pallas_call | solution.py:365
  78.5 0.0 copy-start.1
  78.5 2.3 %copy.7 = f32[3,448,112]{2,1,0:T(8,128)} copy(f32[3,448,112]{1,2,0:T(8,128)} %bitcast.15) | data formatting | bytes 1204224
  80.8 0.0 copy-done.1
  80.8 0.0 copy-start
  80.8 1.1 %copy.8 = f32[3,448,112]{2,1,0:T(8,128)} copy(f32[3,448,112]{1,2,0:T(8,128)S(1)} %bitcast.14) | data formatting | bytes 1204224
  81.9 0.1 copy-done
  82.0 0.9 %copy.10 = bf16[1,1024,448]{1,2,0:T(8,128)(2,1)} copy(bf16[1,1024,448]{1,2,0:T(8,128)(2,1)S(1)} %bitcast.11) | data formatting | bytes 1835008
Async XLA Ops:
  78.5 2.3 %copy-start.1 = (f32[3,112,448]{2,1,0:T(8,128)S(1)}, f32[3,112,448]{2,1,0:T(8,128)}, u32[]{:S(2)}) copy-start(f32[3,112,448]{2,1,0:T(8,128)} %get-tuple-element.8) | copy-start | bytes 1806340
  80.8 1.2 %copy-start = (bf16[448,1024]{1,0:T(8,128)(2,1)S(1)}, bf16[448,1024]{1,0:T(8,128)(2,1)}, u32[]{:S(2)}) copy-start(bf16[448,1024]{1,0:T(8,128)(2,1)} %get-tuple-element.6) | copy-start | bytes 2752516

commit v4 on v3

--- a/solution.py
+++ b/solution.py
@@ -13,7 +13,7 @@
 FIRST_SPACING = 2048
 SECOND_SPACING = 4096
 CHUNKS = 4
-AHEAD = 2
+AHEAD = 3
 
 
 def shifted(block, axis, distance):
@@ -237,9 +237,14 @@
             for copy in move(ch + AHEAD):
                 copy.start()
 
+        @pl.when(ch == CHUNKS - 2)
+        def _():
+            for early in range(CHUNKS - 3):
+                give_back(early).start()
+
         @pl.when(ch == CHUNKS - 1)
         def _():
-            for early in range(CHUNKS - 1):
+            for early in range(CHUNKS - 3, CHUNKS - 1):
                 give_back(early).start()
 
         piece = columns(ch * size, size)
@@ -320,7 +325,7 @@
         copies[4].append(reduce_copy(4, q, s_far.at[span], r_far.at[span], "seq", far))
         copies[4][q].start()
     give_back(CHUNKS - 1).start()
-    outside = jnp.zeros((width, chans), f32)
+    outside = jnp.zeros((chans, width), f32)
     g_two_ref[0] = outside
     g_two_ref[2] = outside
     for q, (start, count) in enumerate(steps):
@@ -337,9 +342,9 @@
         copies[5][q].wait_recv()
         for i, part in enumerate(unpack(r_last[span, :].astype(f32))):
             sums[2 * (1 - parity) + i, span, :] = part
-        for k in range(3):
-            g_one_ref[k, span, :] = sums[k, span, :]
-        g_two_ref[1, span, :] = sums[3, span, :]
+    for k in range(3):
+        g_one_ref[k] = sums[k].T
+    g_two_ref[1] = sums[3].T
 
     for ch in range(CHUNKS):
         give_back(ch).wait()
@@ -366,8 +371,8 @@
         functools.partial(pair_kernel, factor),
         out_shape=(
             jax.ShapeDtypeStruct((chans, positions), bf16),
-            jax.ShapeDtypeStruct((3, width, chans), f32),
-            jax.ShapeDtypeStruct((3, width, chans), f32),
+            jax.ShapeDtypeStruct((3, chans, width), f32),
+            jax.ShapeDtypeStruct((3, chans, width), f32),
         ),
         in_specs=[hbm] * 4,
         out_specs=(vmem, vmem, vmem),
@@ -394,7 +399,7 @@
             collective_id=0, has_side_effects=True, vmem_limit_bytes=62 * 2**20
         ),
     )(inputs[0].T, cotangent[0].T, first_weight_matrix, weight_two)
-    return result.T[None], grad_one.transpose(0, 2, 1), grad_two.transpose(0, 2, 1)
+    return result.T[None], grad_one, grad_two
 
 
 def on_device(inputs, cotangent, first_weight_matrix, weight_two):

time: 83.1 us -> 86 us (1.035)
  Pallas kernels: 77.9 us -> 80.7 us
    pallas_call x1, Pallas kernels: 77.9 us -> 80.7 us  [pair_plan(): pl.pallas_call(functools.partial(pair_kernel, factor), out_shape=(jax.Sha...]
where the time goes in v4:
time: 86 us; the launch traced here: 85.8 us
  Pallas kernels  80.7 us (94%)
  local copies, waits for them, and re-layouts  4.43 us (5%)
    pallas_call x1, Pallas kernels, pair_plan(): pl.pallas_call(functools.partial(pair_kernel, factor), out_shape=(jax.Sha...  80.7 us
    unnamed x7, local copies, waits for them, and re-layouts  4.43 us

profile of v4, /device:TPU:0, one launch (start us, length us, event | category | flops | bytes accessed | tf_op | source)
XLA Modules:
  0.0 85.8 jit_solution(15670488371380260943)
XLA Ops:
  0.6 80.7 %shard_map.67 = (bf16[448,1024]{1,0:T(8,128)(2,1)}, f32[3,448,112]{2,1,0:T(8,128)}, f32[3,448,112]{2,1,0:T(8,128)}) custom-call(bf16[448,1024]{1,0:T(8,128)(2,1)} %bitcast.10, bf16[448,1024]{1,0:T(8,128)(2,1)} %bitcast.11, bf16[3,448,112]{2,1,0:T(8,128)(2,1)} %w1_ref.1, bf16[3,448,112]{2,1,0:T(8,128)(2,1)} %w2_ref.1), custom_call_target="tpu_custom_call" | custom-call | tf_op jit(solution)/shard_map/pallas_call | solution.py:370
  81.4 0.0 copy-start.1
  81.4 2.2 %copy.10 = bf16[1,1024,448]{1,2,0:T(8,128)(2,1)} copy(bf16[1,1024,448]{1,2,0:T(8,128)(2,1)} %bitcast.9) | data formatting | bytes 1835008
  83.6 0.0 copy-done.1
  83.6 0.0 copy-start
  83.6 0.8 copy.11
  84.5 0.5 copy-done
  85.0 0.8 copy.12
Async XLA Ops:
  81.4 2.2 %copy-start.1 = (f32[3,448,112]{2,1,0:T(8,128)S(1)}, f32[3,448,112]{2,1,0:T(8,128)}, u32[]{:S(2)}) copy-start(f32[3,448,112]{2,1,0:T(8,128)} %get-tuple-element.13) | copy-start | bytes 1806340
  83.6 1.3 %copy-start = (f32[3,448,112]{2,1,0:T(8,128)S(1)}, f32[3,448,112]{2,1,0:T(8,128)}, u32[]{:S(2)}) copy-start(f32[3,448,112]{2,1,0:T(8,128)} %get-tuple-element.14) | copy-start | bytes 1806340

commit v5 on v3

--- a/solution.py
+++ b/solution.py
@@ -269,7 +269,7 @@
 
     lax.fori_loop(0, CHUNKS, work, 0)
 
-    steps = [(0, 48), (48, 32), (80, 32)] if width == 112 else [(0, width)]
+    steps = [(0, 64), (64, 48)] if width == 112 else [(0, width)]
 
     def slice_of(owner, start, count):
         owned = pl.ds(pl.multiple_of(owner * width + start, 16), count)

time: 83.1 us -> 85.4 us (1.028)
  Pallas kernels: 77.9 us -> 80.2 us
    pallas_call x1, Pallas kernels: 77.9 us -> 80.2 us  [pair_plan(): pl.pallas_call(functools.partial(pair_kernel, factor), out_shape=(jax.Sha...]
where the time goes in v5:
time: 85.4 us; the launch traced here: 85.2 us
  Pallas kernels  80.2 us (94%)
  local copies, waits for them, and re-layouts  4.39 us (5%)
    pallas_call x1, Pallas kernels, pair_plan(): pl.pallas_call(functools.partial(pair_kernel, factor), out_shape=(jax.Sha...  80.2 us
    unnamed x7, local copies, waits for them, and re-layouts  4.39 us

profile of v5, /device:TPU:0, one launch (start us, length us, event | category | flops | bytes accessed | tf_op | source)
XLA Modules:
  0.0 85.2 jit_solution(7914941270261156752)
XLA Ops:
  0.6 80.2 %shard_map.67 = (bf16[448,1024]{1,0:T(8,128)(2,1)}, f32[3,112,448]{2,1,0:T(8,128)}, f32[3,112,448]{2,1,0:T(8,128)}) custom-call(bf16[448,1024]{1,0:T(8,128)(2,1)} %bitcast.12, bf16[448,1024]{1,0:T(8,128)(2,1)} %bitcast.13, bf16[3,448,112]{2,1,0:T(8,128)(2,1)} %w1_ref.1, bf16[3,448,112]{2,1,0:T(8,128)(2,1)} %w2_ref.1), custom_call_target="tpu_custom_call" | custom-call | tf_op jit(solution)/shard_map/pallas_call | solution.py:365
  80.8 0.0 copy-start.1
  80.8 2.3 %copy.7 = f32[3,448,112]{2,1,0:T(8,128)} copy(f32[3,448,112]{1,2,0:T(8,128)} %bitcast.15) | data formatting | bytes 1204224
  83.1 0.0 copy-done.1
  83.1 0.0 copy-start
  83.1 1.1 %copy.8 = f32[3,448,112]{2,1,0:T(8,128)} copy(f32[3,448,112]{1,2,0:T(8,128)S(1)} %bitcast.14) | data formatting | bytes 1204224
  84.2 0.1 copy-done
  84.3 0.9 %copy.10 = bf16[1,1024,448]{1,2,0:T(8,128)(2,1)} copy(bf16[1,1024,448]{1,2,0:T(8,128)(2,1)S(1)} %bitcast.11) | data formatting | bytes 1835008
Async XLA Ops:
  80.8 2.3 %copy-start.1 = (f32[3,112,448]{2,1,0:T(8,128)S(1)}, f32[3,112,448]{2,1,0:T(8,128)}, u32[]{:S(2)}) copy-start(f32[3,112,448]{2,1,0:T(8,128)} %get-tuple-element.8) | copy-start | bytes 1806340
  83.1 1.2 %copy-start = (bf16[448,1024]{1,0:T(8,128)(2,1)S(1)}, bf16[448,1024]{1,0:T(8,128)(2,1)}, u32[]{:S(2)}) copy-start(bf16[448,1024]{1,0:T(8,128)(2,1)} %get-tuple-element.6) | copy-start | bytes 2752516
